TPU v7x, 32 devices: a whole 2x2x4 slice. The times are simulated.
32 devices in a mesh: groups: 2 (over x), tensor: 16 (over z, y, core).
Axes of the slice: x: 2, y: 2, z: 4, core: 2. Of those that a mesh axis runs over, the one named last changes fastest.
Arguments:
- hidden: bfloat16 [384, 16384], P('groups', 'tensor'), parts along dimension 0, may hold values from -6 to 6
- w_query: bfloat16 [16384, 8192], P(None, 'tensor'), may hold values from -0.046875 to 0.046875
- w_out: bfloat16 [8192, 16384], P('tensor'), may hold values from -0.09375 to 0.09375
- new_kv: bfloat16 [384, 2, 4, 128], P(('groups', 'tensor')), parts along dimension 0, may hold values from -6 to 6
- prefix_kv: bfloat16 [32, 3, 2, 4, 512, 128], P(('groups', 'tensor')), parts along dimension 0, may hold values from -700 to 700
- suffix_kv: bfloat16 [384, 2, 4, 256, 128], P(('groups', 'tensor')), parts along dimension 0, may hold values from -6 to 6
- parents: int32 [384], P(('groups', 'tensor')), parts along dimension 0, may hold values from 0 to 7
- lengths: int32 [384], P(('groups', 'tensor')), parts along dimension 0, may hold values from 1 to 256, 36864 in all
Outputs:
- attended: bfloat16 [384, 16384], P('groups', 'tensor'), parts along dimension 0
There are 2 independent parts, one for each index of `groups`. A program takes and returns all parts, laid end to end along the dimension named above; an argument that names none is the same for every part. Nothing has to cross between parts.
Inputs may be any that keep to these rules, and one draw needn't show every extreme that they name: `lengths`: some page is full.
All inputs are finite; a program needn't handle non-finite values. No bound on the sum of `lengths` on one device may be relied on, other than what follows from the above.
Results may differ from a plain program's by a relative error of at most 0.02.
The roundings to bfloat16 on the way count: a program that leaves them out, or rounds other values in their place, can miss the bound.
Values may be sent and summed in bfloat16 or wider, within the bound.
No kernel may reach another device: no remote copies, remote signals or barrier semaphores. Data moves between devices by JAX's collectives and lax.ppermute only.
A program may use at most 192 MiB of HBM per device.

v0:
```python
import jax
import jax.numpy as jnp
from jax import lax
from jax.sharding import PartitionSpec as P

HEADS = 64
KV = 4
HD = 128
BEAMS = 8
big_negative = -1e30
rope_base = 500000.0


def swapped(block, axis, apart):
    count = lax.axis_size(axis)
    route = []
    for low in range(count):
        high = low | 1 << apart
        if high != low and high < count:
            route += [(low, high), (high, low)]
    return lax.ppermute(block, axis, route)


def rotate(queries, position):
    half_size = HD // 2
    frequency = rope_base ** (-jnp.arange(half_size, dtype=jnp.float32) * 2.0 / HD)
    angles = position.astype(jnp.float32)[..., None, None] * frequency
    cosine = jnp.cos(angles)
    sines = jnp.sin(angles)
    entries = queries.astype(jnp.float32)
    lower_half = entries[..., :half_size]
    upper_half = entries[..., half_size:]
    turned = jnp.concatenate(
        [lower_half * cosine - upper_half * sines, upper_half * cosine + lower_half * sines],
        axis=-1,
    )
    return (turned * HD ** (-0.5)).astype(jnp.bfloat16)


def shared_part(grouped, key_block, value_block):
    scores = jnp.einsum("pbkge,pkne->pbkgn", grouped, key_block, preferred_element_type=jnp.float32)
    highest = jnp.max(scores, axis=-1)
    weights = jnp.exp(scores - highest[..., None])
    weight_sum = jnp.sum(weights, axis=-1)
    weighted = jnp.einsum(
        "pbkgn,pkne->pbkge",
        weights.astype(jnp.bfloat16),
        value_block,
        preferred_element_type=jnp.float32,
    )
    return (highest, weight_sum, weighted)


def own_part(grouped, key_block, value_block, usable):
    scores = jnp.einsum(
        "pbkge,pbkse->pbkgs", grouped, key_block, preferred_element_type=jnp.float32
    )
    usable_mask = usable[:, :, None, None, :]
    highest = jnp.max(jnp.where(usable_mask, scores, big_negative), axis=-1)
    weights = jnp.where(usable_mask, jnp.exp(scores - highest[..., None]), 0.0)
    weight_sum = jnp.sum(weights, axis=-1)
    weighted = jnp.einsum(
        "pbkgs,pbkse->pbkge",
        weights.astype(jnp.bfloat16),
        value_block,
        preferred_element_type=jnp.float32,
    )
    return (highest, weight_sum, weighted)


def combine(left_state, right_state):
    highest = jnp.maximum(left_state[0], right_state[0])
    left_factor = jnp.exp(left_state[0] - highest)
    right_factor = jnp.exp(right_state[0] - highest)
    weight_sum = left_state[1] * left_factor + right_state[1] * right_factor
    weighted = left_state[2] * left_factor[..., None] + right_state[2] * right_factor[..., None]
    return (highest, weight_sum, weighted)


def body(hidden, w_query, w_out, new_kv, prefix_kv, suffix_kv, parents, lengths):
    pair_side = lax.axis_index("tensor") % 2
    rows_here = new_kv.shape[0]
    half_beams = BEAMS // 2
    prompts_here = rows_here // half_beams
    prefix_len = 2 * prefix_kv.shape[4]
    page_size = suffix_kv.shape[3]
    per_kv = HEADS // KV

    def in_order(own_part_rows, far_rows, along):
        lower_part = jnp.where(pair_side == 0, own_part_rows, far_rows)
        upper_part = jnp.where(pair_side == 0, far_rows, own_part_rows)
        return jnp.concatenate([lower_part, upper_part], axis=along)

    query = jnp.dot(
        lax.all_gather(hidden, "tensor", axis=1, tiled=True),
        w_query,
        preferred_element_type=jnp.float32,
    ).astype(jnp.bfloat16)
    local_q = lax.all_to_all(query, "tensor", split_axis=0, concat_axis=1, tiled=True)
    local_q = local_q.reshape(prompts_here, half_beams, HEADS, HD)
    own_par = parents.reshape(prompts_here, half_beams)
    own_len = lengths.reshape(prompts_here, half_beams)
    own_pages = suffix_kv.reshape(prompts_here, half_beams, 2, KV, page_size, HD)
    new_pair = new_kv.reshape(prompts_here, half_beams, 2, KV, HD)
    positions = jnp.arange(page_size)
    far_prefix, far_pages, far_len = swapped((prefix_kv, suffix_kv, lengths), "tensor", 0)
    prefix_full = in_order(prefix_kv[0], far_prefix[0], 3)
    pages_all = in_order(own_pages, far_pages.reshape(own_pages.shape), 1)
    len_all = in_order(own_len, far_len.reshape(own_len.shape), 1)
    chosen = jnp.take_along_axis(pages_all, own_par[:, :, None, None, None, None], axis=1)
    page_len = jnp.take_along_axis(len_all, own_par, axis=1)
    grouped = rotate(local_q, prefix_len + page_len).reshape(
        prompts_here, half_beams, KV, per_kv, HD
    )
    prefix_state = shared_part(grouped, prefix_full[:, 0], prefix_full[:, 1])
    usable = positions[None, None, :] < page_len[:, :, None]
    suffix_state = own_part(grouped, chosen[:, :, 0], chosen[:, :, 1], usable)
    merged = combine(prefix_state, suffix_state)
    new_scores = jnp.einsum(
        "pbkge,pbke->pbkg", grouped, new_pair[:, :, 0], preferred_element_type=jnp.float32
    )
    new_values = jnp.broadcast_to(
        new_pair[:, :, 1].astype(jnp.float32)[:, :, :, None, :], grouped.shape
    )
    new_state = (new_scores, jnp.ones_like(new_scores), new_values)
    highest, weight_sum, weighted = combine(merged, new_state)
    heads_out = (
        (weighted / weight_sum[..., None]).astype(jnp.bfloat16).reshape(rows_here, HEADS * HD)
    )
    heads_view = lax.all_to_all(heads_out, "tensor", split_axis=1, concat_axis=0, tiled=True)
    projected = jnp.dot(heads_view, w_out, preferred_element_type=jnp.float32)
    summed = lax.psum_scatter(
        projected.astype(jnp.bfloat16), "tensor", scatter_dimension=1, tiled=True
    )
    return summed


def solution(mesh):
    return jax.shard_map(
        body,
        mesh=mesh,
        in_specs=(
            P("groups", "tensor"),
            P(None, "tensor"),
            P("tensor", None),
            P(("groups", "tensor"), None, None, None),
            P(("groups", "tensor"), None, None, None, None, None),
            P(("groups", "tensor"), None, None, None, None),
            P(("groups", "tensor")),
            P(("groups", "tensor")),
        ),
        out_specs=P("groups", "tensor"),
        check_vma=False,
    )
```

profile of v0, /device:TPU:0, one launch (start us, length us, event | category | flops | bytes accessed | tf_op | source)
XLA Modules:
  0.0 227.0 jit_solution(14612947954421246856)
XLA Ops:
  6.6 0.7 all-gather.2.cloned.1.call-update
  7.3 0.5 collective-permute-start.2
  7.8 3.9 %copy.48 = bf16[1,3,2,4,512,128]{5,4,3,1,2,0:T(8,128)(2,1)} copy(bf16[1,3,2,4,512,128]{5,4,3,2,1,0:T(8,128)(2,1)} %param.12) | data formatting | bytes 6291456 | tf_op args[4]
  11.6 0.2 collective-permute-start
  11.8 0.3 collective-permute-start.1
  12.2 0.1 reshape.192
  12.2 0.1 reshape.191
  12.3 0.1 reshape.196
  12.4 0.6 fusion.75
  13.1 0.6 fusion.67
  13.7 3.9 %collective-permute-done.1 = s32[12]{0:T(128)S(1)} collective-permute-done((s32[12]{0:T(128)S(1)}, s32[12]{0:T(128)S(1)}, u32[]{:S(2)}, u32[]{:S(2)}) %collective-permute-start.1) | collective-permute-done | bytes 80 | tf_op jit(solution)/shard_map/ppermute | solution.py:21
  17.6 0.1 select_n.128
  17.7 0.1 select_n.126
  17.7 0.1 pad_add_fusion
  17.8 0.7 gather_fusion
  18.6 0.1 reshape.199
  18.7 0.1 iota_compare_fusion
  18.7 0.7 multiply_cosine_fusion
  19.5 3.0 %collective-permute-done = bf16[1,3,2,4,512,128]{5,4,3,1,2,0:T(8,128)(2,1)} collective-permute-done((bf16[1,3,2,4,512,128]{5,4,3,1,2,0:T(8,128)(2,1)}, bf16[1,3,2,4,512,128]{5,4,3,1,2,0:T(8,128)(2,1)}, u32[]{:S(2)}, u32[]{:S(2)}) %collective-permute-start) | collective-permute-done | bytes 3145760 | tf_op jit(solution)/shard_map/ppermute | solution.py:21
  22.4 5.0 %select_bitcast_fusion.1 = (bf16[3,2,4,512,128]{4,3,2,0,1:T(8,128)(2,1)}, bf16[3,2,4,512,128]{4,3,2,0,1:T(8,128)(2,1)}) fusion(bf16[1,3,2,4,512,128]{5,4,3,1,2,0:T(8,128)(2,1)} %collective-permute-done, pred[]{:T(512)S(6)} %eq.4, bf16[1,3,2,4,512,128]{5,4,3,2,1,0:T(8,128)(2,1)S(1)} %copy-done), kind=kLoop, calls=%fused_computation.24 | loop fusion | flops 3145728 | bytes 12582913 | tf_op jit(solution)/shard_map/jit(_where)/select_n | solution.py:90
  27.5 3.9 %broadcast_select_fusion.1 = (bf16[12,2,4,256,128]{4,3,2,1,0:T(8,128)(2,1)S(1)}, bf16[12,2,4,256,128]{4,3,2,1,0:T(8,128)(2,1)S(1)}) fusion(bf16[12,2,4,256,128]{4,3,2,1,0:T(8,128)(2,1)S(1)} %bitcast.116, bf16[12,2,4,256,128]{4,3,2,1,0:T(8,128)(2,1)} %collective-permute-done.2, pred[]{:T(512)S(6)} %eq.4), kind=kLoop, calls=%fused_computation.7 | loop fusion | flops 6291456 | bytes 25165824 | tf_op jit(solution)/shard_map/jit(_where)/select_n | solution.py:90
  31.4 5.3 %pad_maximum_fusion = bf16[3,8,2,4,256,128]{5,4,3,2,1,0:T(8,128)(2,1)} fusion(bf16[3,4,2,4,256,128]{5,4,3,2,1,0:T(8,128)(2,1)S(1)} %bitcast.112, bf16[3,4,2,4,256,128]{5,4,3,2,1,0:T(8,128)(2,1)S(1)} %bitcast.111), kind=kLoop, calls=%fused_computation.3 | loop fusion | flops 6291456 | bytes 25165824 | tf_op jit(solution)/shard_map/concatenate | solution.py:92
  36.6 8.8 %gather_fusion.1 = bf16[12,2,4,256,128]{4,3,2,1,0:T(8,128)(2,1)} fusion(bf16[3,8,2,4,256,128]{5,4,3,2,1,0:T(8,128)(2,1)} %pad_maximum_fusion, s32[12]{0:T(128)S(1)} %reshape.196), kind=kCustom, calls=%fused_computation.1 | custom fusion | bytes 12583008 | tf_op jit(solution)/shard_map/jit(take_along_axis)/gather | solution.py:110
  45.4 6.2 %copy.53 = bf16[12,2,4,256,128]{4,3,2,0,1:T(8,128)(2,1)} copy(bf16[12,2,4,256,128]{4,3,2,1,0:T(8,128)(2,1)} %gather_fusion.1) | data formatting | bytes 12582912 | tf_op jit(solution)/shard_map/jit(take_along_axis)/gather | solution.py:110
  51.7 22.6 %all-gather.2.cloned.1.call-done = bf16[192,16384]{1,0:T(8,128)(2,1)} async-done(((bf16[192,1024]{1,0:T(8,128)(2,1)}), bf16[192,16384]{1,0:T(8,128)(2,1)}) %all-gather.2.cloned.1.call-update) | async-done | bytes 6291472 | tf_op jit(solution)/shard_map/all_gather | solution.py:95
  74.2 11.0 %convolution_convert_fusion.1 = bf16[192,512]{1,0:T(8,128)(2,1)S(1)} fusion(bf16[192,16384]{1,0:T(8,128)(2,1)} %all-gather.2.cloned.1.call-done, bf16[16384,512]{1,0:T(8,128)(2,1)} %param.9), kind=kOutput, calls=%fused_computation.35 | convolution fusion | flops 3221323776 | bytes 23265280 | tf_op jit(solution)/shard_map/dot_general | solution.py:94
  85.2 0.7 all_to_all.24
  86.0 3.5 %all-to-all-start = ((bf16[16,12,512]{2,1,0:T(8,128)(2,1)}), bf16[16,12,512]{2,1,0:T(8,128)(2,1)S(1)}, u32[]{:S(2)}, u32[]{:S(2)}) async-start(bf16[16,12,512]{2,1,0:T(8,128)(2,1)} %all_to_all.24), calls=%async_computation | async-start | bytes 524288 | tf_op jit(solution)/shard_map/all_to_all | solution.py:99
  89.5 0.0 reduce-scatter.2.cloned.1.call-start
  89.6 6.1 %broadcast_select_fusion.2 = bf16[3,4,2,4,256,128]{5,4,3,1,0,2:T(8,128)(2,1)} fusion(bf16[3,4,2,4,256,128]{5,4,3,1,0,2:T(8,128)(2,1)} %bitcast.110, pred[3,4]{1,0:T(4,128)(4,1)S(1)} %get-tuple-element.12), kind=kLoop, calls=%fused_computation.8 | loop fusion | flops 3145728 | bytes 12582924 | tf_op jit(solution)/shard_map/jit(take_along_axis)/select_n | solution.py:110
  95.7 3.8 %all-to-all-done = bf16[16,12,512]{2,1,0:T(8,128)(2,1)S(1)} async-done(((bf16[16,12,512]{2,1,0:T(8,128)(2,1)}), bf16[16,12,512]{2,1,0:T(8,128)(2,1)S(1)}, u32[]{:S(2)}, u32[]{:S(2)}) %all-to-all-start) | async-done | bytes 196640 | tf_op jit(solution)/shard_map/all_to_all | solution.py:99
  99.6 1.0 copy.50
  100.6 1.0 reshape.194
  101.6 1.0 multiply_subtract_fusion
  102.6 0.2 fusion.56
  102.8 0.9 fusion.58
  103.7 2.9 %select_reduce_fusion = (f32[3,4,4,16]{3,2,1,0:T(4,128)S(1)}, f32[3,4,4,16,256]{4,3,2,1,0:T(8,128)S(1)}) fusion(pred[3,4,256]{2,1,0:T(4,128)(4,1)S(1)} %iota_compare_fusion, bf16[3,4,2,4,256,128]{5,4,3,1,0,2:T(8,128)(2,1)} %broadcast_select_fusion.2, bf16[3,4,4,16,128]{4,3,1,2,0:T(8,128)(2,1)S(1)} %fusion.56), kind=kOutput, calls=%fused_computation.39 | convolution fusion | flops 50724096 | bytes 4134912 | tf_op jit(solution)/shard_map/pbkge,pbkse->pbkgs/dot_general | solution.py:55
  106.7 0.4 fusion.54
  107.0 1.3 bitcast_reduce_fusion
  108.4 0.7 fusion.12
  109.1 0.5 slice-done.1
  109.6 0.5 fusion.21
  110.2 1.3 fusion.49
  111.4 0.1 all_to_all.26
  111.6 0.1 copy.61
  111.7 12.8 %all_to_all.32 = bf16[12,16,512]{2,0,1:T(8,128)(2,1)S(1)} all-to-all(bf16[12,16,512]{2,0,1:T(8,128)(2,1)S(1)} %copy.61), channel_id=1, replica_groups=mesh['groups'=2,'tensor'=16] {'tensor'}, dimensions={1} | all-to-all | bytes 393216 | tf_op jit(solution)/shard_map/all_to_all | solution.py:130
  124.6 11.9 %convolution_convert_fusion = bf16[192,16384]{1,0:T(8,128)(2,1)} fusion(bf16[192,512]{1,0:T(8,128)(2,1)S(1)} %all_to_all.29, bf16[512,16384]{1,0:T(8,128)(2,1)} %param.10), kind=kOutput, calls=%fused_computation.2 | convolution fusion | flops 3224371200 | bytes 23265280 | tf_op jit(solution)/shard_map/dot_general | solution.py:131
  136.5 83.7 %reduce-scatter.2.cloned.1.call-done = bf16[192,1024]{1,0:T(8,128)(2,1)} async-done(((bf16[192,16384]{1,0:T(8,128)(2,1)}), bf16[192,1024]{1,0:T(8,128)(2,1)}) %reduce-scatter.2.cloned.1.call-update) | async-done | bytes 393232 | tf_op jit(solution)/shard_map/reduce_scatter | solution.py:132
  (34 shorter events, 0.3 us)
Async XLA Ops:
  6.5 15.9 %copy-start = (bf16[1,3,2,4,512,128]{5,4,3,2,1,0:T(8,128)(2,1)S(1)}, bf16[1,3,2,4,512,128]{5,4,3,2,1,0:T(8,128)(2,1)}, u32[]{:S(2)}) copy-start(bf16[1,3,2,4,512,128]{5,4,3,2,1,0:T(8,128)(2,1)} %param.12) | copy-start | bytes 9437188
  6.5 5.3 %copy-start.6 = (s32[12]{0:T(128)S(1)}, s32[12]{0:T(128)}, u32[]{:S(2)}) copy-start(s32[12]{0:T(128)} %param.15) | copy-start | bytes 148
  6.5 5.6 %copy-start.5 = (s32[12]{0:T(128)S(1)}, s32[12]{0:T(128)}, u32[]{:S(2)}) copy-start(s32[12]{0:T(128)} %param.14) | copy-start | bytes 148
  6.5 5.9 %copy-start.3 = (bf16[12,2,4,128]{3,2,1,0:T(4,128)(2,1)S(1)}, bf16[12,2,4,128]{3,2,1,0:T(4,128)(2,1)}, u32[]{:S(2)}) copy-start(bf16[12,2,4,128]{3,2,1,0:T(4,128)(2,1)} %param.11) | copy-start | bytes 73732
  6.5 67.7 %all-gather.2.cloned.1.call-start = ((), (), s32[]{:S(2)}) async-start(), calls=%async_computation.3 | async-start | bytes 6684672 | tf_op jit(solution)/shard_map/all_gather | solution.py:95
  7.3 20.2 %collective-permute-start.2 = (bf16[12,2,4,256,128]{4,3,2,1,0:T(8,128)(2,1)}, bf16[12,2,4,256,128]{4,3,2,1,0:T(8,128)(2,1)}, u32[]{:S(2)}, u32[]{:S(2)}) collective-permute-start(bf16[12,2,4,256,128]{4,3,2,1,0:T(8,128)(2,1)} %param.13), channel_id=1, source_target_pairs={{0,1},{1,0},{2,3},{3,2},{4,5},{5,4},{6,7},{7,6},{8,9},{9,8},{10,11... | collective-permute-start | bytes 18874376 | tf_op jit(solution)/shard_map/ppermute | solution.py:21
  11.6 10.8 %collective-permute-start = (bf16[1,3,2,4,512,128]{5,4,3,1,2,0:T(8,128)(2,1)}, bf16[1,3,2,4,512,128]{5,4,3,1,2,0:T(8,128)(2,1)}, u32[]{:S(2)}, u32[]{:S(2)}) collective-permute-start(bf16[1,3,2,4,512,128]{5,4,3,1,2,0:T(8,128)(2,1)} %copy.48), channel_id=1, source_target_pairs={{0,1},{1,0},{2,3},{3,2},{4,5},{5,4},{6,7},{7,6},{8,9},{9,8},{10,11... | collective-permute-start | bytes 9437192 | tf_op jit(solution)/shard_map/ppermute | solution.py:21
  11.8 5.7 %collective-permute-start.1 = (s32[12]{0:T(128)S(1)}, s32[12]{0:T(128)S(1)}, u32[]{:S(2)}, u32[]{:S(2)}) collective-permute-start(s32[12]{0:T(128)S(1)} %copy-done.6), channel_id=1, source_target_pairs={{0,1},{1,0},{2,3},{3,2},{4,5},{5,4},{6,7},{7,6},{8,9},{9,8},{10,11... | collective-permute-start | bytes 152 | tf_op jit(solution)/shard_map/ppermute | solution.py:21
  18.7 8.7 %slice-start.2 = ((s8[6291456]{0:T(1024)(128)(4,1)}), s8[4194304]{0:T(1024)(128)(4,1)S(1)}, s32[]{:S(2)}) async-start(s8[6291456]{0:T(1024)(128)(4,1)} %bitcast.115), calls=%async_computation.7 | async-start | bytes 8388608
  19.5 8.0 %slice-start.3 = ((s8[6291456]{0:T(1024)(128)(4,1)}), s8[2097152]{0:T(1024)(128)(4,1)S(1)}, s32[]{:S(2)}) async-start(s8[6291456]{0:T(1024)(128)(4,1)} %bitcast.115), calls=%async_computation.8 | async-start | bytes 4194304
  86.0 13.5 %all-to-all-start = ((bf16[16,12,512]{2,1,0:T(8,128)(2,1)}), bf16[16,12,512]{2,1,0:T(8,128)(2,1)S(1)}, u32[]{:S(2)}, u32[]{:S(2)}) async-start(bf16[16,12,512]{2,1,0:T(8,128)(2,1)} %all_to_all.24), calls=%async_computation | async-start | bytes 524288 | tf_op jit(solution)/shard_map/all_to_all | solution.py:99
  89.5 130.6 %reduce-scatter.2.cloned.1.call-start = ((), (), s32[]{:S(2)}) async-start(), calls=%async_computation.4 | async-start | bytes 6684672 | tf_op jit(solution)/shard_map/reduce_scatter | solution.py:132
  95.7 11.3 %copy-start.1 = (bf16[3,2,4,512,128]{4,3,2,0,1:T(8,128)(2,1)S(1)}, bf16[3,2,4,512,128]{4,3,2,0,1:T(8,128)(2,1)}, u32[]{:S(2)}) copy-start(bf16[3,2,4,512,128]{4,3,2,0,1:T(8,128)(2,1)} %get-tuple-element.15) | copy-start | bytes 9437188
  101.6 5.4 %copy-start.2 = (bf16[3,2,4,512,128]{4,3,2,0,1:T(8,128)(2,1)S(1)}, bf16[3,2,4,512,128]{4,3,2,0,1:T(8,128)(2,1)}, u32[]{:S(2)}) copy-start(bf16[3,2,4,512,128]{4,3,2,0,1:T(8,128)(2,1)} %get-tuple-element.16) | copy-start | bytes 9437188
  106.6 2.5 %slice-start = ((s8[6291456]{0:T(1024)(128)(4,1)}), s8[4194304]{0:T(1024)(128)(4,1)S(1)}, s32[]{:S(2)}) async-start(s8[6291456]{0:T(1024)(128)(4,1)} %bitcast.113), calls=%async_computation.5 | async-start | bytes 8388608
  107.0 2.6 %slice-start.1 = ((s8[6291456]{0:T(1024)(128)(4,1)}), s8[2097152]{0:T(1024)(128)(4,1)S(1)}, s32[]{:S(2)}) async-start(s8[6291456]{0:T(1024)(128)(4,1)} %bitcast.113), calls=%async_computation.6 | async-start | bytes 4194304
  108.4 1.8 copy-start.4
Sparse Core Ops, SparseCore 0:
  9.6 64.6 all-gather.1
  136.6 83.5 reduce-scatter.1
where the time goes:
time: 228 us; the launch traced here: 227 us
  waiting for transfers between devices  118 us (52%)
  matrix products  29.8 us (13%)
  local copies, waits for them, and re-layouts  24.4 us (11%)
  other arithmetic  24.1 us (11%)
  between operations  13.6 us (6%)
  blocking collectives  12.8 us (6%)
  starting transfers between devices  4.64 us (2%)
    reduce_scatter x1, waiting for transfers between devices, body(): lax.psum_scatter(projected.astype(jnp.bfloat16), 'tensor', scatter_dimens...  83.7 us
    all_gather x1, waiting for transfers between devices, body(): lax.all_gather(hidden, 'tensor', axis=1, tiled=True)  22.6 us
    gather x2, local copies, waits for them, and re-layouts, body(): jnp.take_along_axis(pages_all, own_par[:, :, None, None, None, None], axi...  15 us
    all_to_all x1, blocking collectives, body(): lax.all_to_all(heads_out, 'tensor', split_axis=1, concat_axis=0, tiled=True)  12.8 us
    dot_general x1, matrix products, body(): projected = jnp.dot(heads_view, w_out, preferred_element_type=jnp.float32)  11.9 us
    dot_general x1, matrix products, body(): jnp.dot(lax.all_gather(hidden, 'tensor', axis=1, tiled=True), w_query, pr...  11 us
    select_n x3, other arithmetic, in_order(): lower_part = jnp.where(pair_side == 0, own_part_rows, far_rows)  8.91 us
    ppermute x3, waiting for transfers between devices, swapped(): return lax.ppermute(block, axis, route)  6.88 us
  transfers between devices with their start and end apart: 6, of which 5 were waited for; matrix products, arithmetic and copies ran while one was open for 19% of the time, Pallas kernels for 0%

commit v1 on v0

--- a/solution.py
+++ b/solution.py
@@ -96,7 +96,10 @@
         w_query,
         preferred_element_type=jnp.float32,
     ).astype(jnp.bfloat16)
-    local_q = lax.all_to_all(query, "tensor", split_axis=0, concat_axis=1, tiled=True)
+    count_2 = lax.axis_size("tensor")
+    pieces = jnp.stack(jnp.split(query, count_2, axis=0), axis=0)
+    pieces = lax.all_to_all(pieces, "tensor", split_axis=0, concat_axis=0)
+    local_q = jnp.concatenate(pieces, axis=1)
     local_q = local_q.reshape(prompts_here, half_beams, HEADS, HD)
     own_par = parents.reshape(prompts_here, half_beams)
     own_len = lengths.reshape(prompts_here, half_beams)

time: 228 us -> 237 us (1.039)
  local copies, waits for them, and re-layouts: 24.4 us -> 33.3 us
    unnamed x23 -> x38, local copies, waits for them, and re-layouts: 4.41 us -> 13.5 us
  transfers between devices with their start and end apart: 6 -> 6, of which waited for: 5 -> 5; matrix products, arithmetic and copies ran while one was open for 19% -> 18% of each run, Pallas kernels for 0% -> 0%
where the time goes in v1:
time: 237 us; the launch traced here: 236 us
  waiting for transfers between devices  118 us (50%)
  local copies, waits for them, and re-layouts  33.3 us (14%)
  matrix products  29.8 us (13%)
  other arithmetic  24.1 us (10%)
  between operations  13.6 us (6%)
  blocking collectives  12.8 us (5%)
  starting transfers between devices  4.64 us (2%)
    reduce_scatter x1, waiting for transfers between devices, body(): lax.psum_scatter(projected.astype(jnp.bfloat16), 'tensor', scatter_dimens...  83.7 us
    all_gather x1, waiting for transfers between devices, body(): lax.all_gather(hidden, 'tensor', axis=1, tiled=True)  22.6 us
    gather x2, local copies, waits for them, and re-layouts, body(): jnp.take_along_axis(pages_all, own_par[:, :, None, None, None, None], axi...  15 us
    unnamed x38, local copies, waits for them, and re-layouts  13.5 us
    all_to_all x1, blocking collectives, body(): lax.all_to_all(heads_out, 'tensor', split_axis=1, concat_axis=0, tiled=True)  12.8 us
    dot_general x1, matrix products, body(): projected = jnp.dot(heads_view, w_out, preferred_element_type=jnp.float32)  11.9 us
    dot_general x1, matrix products, body(): jnp.dot(lax.all_gather(hidden, 'tensor', axis=1, tiled=True), w_query, pr...  11 us
    select_n x3, other arithmetic, in_order(): lower_part = jnp.where(pair_side == 0, own_part_rows, far_rows)  8.91 us
  transfers between devices with their start and end apart: 6, of which 5 were waited for; matrix products, arithmetic and copies ran while one was open for 18% of the time, Pallas kernels for 0%

profile of v1, /device:TPU:0, one launch (start us, length us, event | category | flops | bytes accessed | tf_op | source)
XLA Modules:
  0.0 236.0 jit_solution(11216684473308494828)
XLA Ops:
  6.6 0.7 all-gather.2.cloned.1.call-update
  7.3 0.5 collective-permute-start.2
  7.8 3.9 %copy.48 = bf16[1,3,2,4,512,128]{5,4,3,1,2,0:T(8,128)(2,1)} copy(bf16[1,3,2,4,512,128]{5,4,3,2,1,0:T(8,128)(2,1)} %param.12) | data formatting | bytes 6291456 | tf_op args[4]
  12.4 0.6 fusion.75
  13.1 0.6 fusion.67
  13.7 3.9 %collective-permute-done.1 = s32[12]{0:T(128)S(1)} collective-permute-done((s32[12]{0:T(128)S(1)}, s32[12]{0:T(128)S(1)}, u32[]{:S(2)}, u32[]{:S(2)}) %collective-permute-start.1) | collective-permute-done | bytes 80 | tf_op jit(solution)/shard_map/ppermute | solution.py:21
  17.8 0.7 gather_fusion
  18.7 0.7 multiply_cosine_fusion
  19.5 3.0 %collective-permute-done = bf16[1,3,2,4,512,128]{5,4,3,1,2,0:T(8,128)(2,1)} collective-permute-done((bf16[1,3,2,4,512,128]{5,4,3,1,2,0:T(8,128)(2,1)}, bf16[1,3,2,4,512,128]{5,4,3,1,2,0:T(8,128)(2,1)}, u32[]{:S(2)}, u32[]{:S(2)}) %collective-permute-start) | collective-permute-done | bytes 3145760 | tf_op jit(solution)/shard_map/ppermute | solution.py:21
  22.4 5.0 %select_bitcast_fusion.1 = (bf16[3,2,4,512,128]{4,3,2,0,1:T(8,128)(2,1)}, bf16[3,2,4,512,128]{4,3,2,0,1:T(8,128)(2,1)}) fusion(bf16[1,3,2,4,512,128]{5,4,3,1,2,0:T(8,128)(2,1)} %collective-permute-done, pred[]{:T(512)S(6)} %eq.4, bf16[1,3,2,4,512,128]{5,4,3,2,1,0:T(8,128)(2,1)S(1)} %copy-done), kind=kLoop, calls=%fused_computation.24 | loop fusion | flops 3145728 | bytes 12582913 | tf_op jit(solution)/shard_map/jit(_where)/select_n | solution.py:90
  27.5 3.9 %broadcast_select_fusion.1 = (bf16[12,2,4,256,128]{4,3,2,1,0:T(8,128)(2,1)S(1)}, bf16[12,2,4,256,128]{4,3,2,1,0:T(8,128)(2,1)S(1)}) fusion(bf16[12,2,4,256,128]{4,3,2,1,0:T(8,128)(2,1)S(1)} %bitcast.180, bf16[12,2,4,256,128]{4,3,2,1,0:T(8,128)(2,1)} %collective-permute-done.2, pred[]{:T(512)S(6)} %eq.4), kind=kLoop, calls=%fused_computation.7 | loop fusion | flops 6291456 | bytes 25165824 | tf_op jit(solution)/shard_map/jit(_where)/select_n | solution.py:90
  31.4 5.3 %pad_maximum_fusion = bf16[3,8,2,4,256,128]{5,4,3,2,1,0:T(8,128)(2,1)} fusion(bf16[3,4,2,4,256,128]{5,4,3,2,1,0:T(8,128)(2,1)S(1)} %bitcast.176, bf16[3,4,2,4,256,128]{5,4,3,2,1,0:T(8,128)(2,1)S(1)} %bitcast.175), kind=kLoop, calls=%fused_computation.3 | loop fusion | flops 6291456 | bytes 25165824 | tf_op jit(solution)/shard_map/concatenate | solution.py:92
  36.6 8.8 %gather_fusion.1 = bf16[12,2,4,256,128]{4,3,2,1,0:T(8,128)(2,1)} fusion(bf16[3,8,2,4,256,128]{5,4,3,2,1,0:T(8,128)(2,1)} %pad_maximum_fusion, s32[12]{0:T(128)S(1)} %reshape.192), kind=kCustom, calls=%fused_computation.1 | custom fusion | bytes 12583008 | tf_op jit(solution)/shard_map/jit(take_along_axis)/gather | solution.py:113
  45.4 6.2 %copy.53 = bf16[12,2,4,256,128]{4,3,2,0,1:T(8,128)(2,1)} copy(bf16[12,2,4,256,128]{4,3,2,1,0:T(8,128)(2,1)} %gather_fusion.1) | data formatting | bytes 12582912 | tf_op jit(solution)/shard_map/jit(take_along_axis)/gather | solution.py:113
  51.7 22.6 %all-gather.2.cloned.1.call-done = bf16[192,16384]{1,0:T(8,128)(2,1)} async-done(((bf16[192,1024]{1,0:T(8,128)(2,1)}), bf16[192,16384]{1,0:T(8,128)(2,1)}) %all-gather.2.cloned.1.call-update) | async-done | bytes 6291472 | tf_op jit(solution)/shard_map/all_gather | solution.py:95
  74.2 11.0 %convolution_convert_fusion.1 = bf16[192,512]{1,0:T(8,128)(2,1)S(1)} fusion(bf16[192,16384]{1,0:T(8,128)(2,1)} %all-gather.2.cloned.1.call-done, bf16[16384,512]{1,0:T(8,128)(2,1)} %param.9), kind=kOutput, calls=%fused_computation.35 | convolution fusion | flops 3221323776 | bytes 23265280 | tf_op jit(solution)/shard_map/dot_general | solution.py:94
  85.2 0.6 constant_dynamic-update-slice_fusion.15
  85.8 0.6 constant_dynamic-update-slice_fusion.14
  86.5 0.6 constant_dynamic-update-slice_fusion.13
  87.1 0.6 constant_dynamic-update-slice_fusion.12
  87.7 0.6 constant_dynamic-update-slice_fusion.11
  88.3 0.6 constant_dynamic-update-slice_fusion.10
  88.9 0.6 constant_dynamic-update-slice_fusion.9
  89.5 0.6 constant_dynamic-update-slice_fusion.8
  90.1 0.6 constant_dynamic-update-slice_fusion.7
  90.7 0.6 constant_dynamic-update-slice_fusion.6
  91.3 0.6 constant_dynamic-update-slice_fusion.5
  91.9 0.6 constant_dynamic-update-slice_fusion.4
  92.5 0.6 constant_dynamic-update-slice_fusion.3
  93.2 0.6 constant_dynamic-update-slice_fusion.2
  93.8 0.6 constant_dynamic-update-slice_fusion.1
  94.4 0.6 constant_dynamic-update-slice_fusion
  95.0 3.5 %all-to-all-start = ((bf16[16,12,512]{2,1,0:T(8,128)(2,1)}), bf16[16,12,512]{2,1,0:T(8,128)(2,1)S(1)}, u32[]{:S(2)}, u32[]{:S(2)}) async-start(bf16[16,12,512]{2,1,0:T(8,128)(2,1)} %constant_dynamic-update-slice_fusion), calls=%async_computation | async-start | bytes 524288 | tf_op jit(solution)/shard_map/all_to_all | solution.py:101
  98.6 6.1 %broadcast_select_fusion.2 = bf16[3,4,2,4,256,128]{5,4,3,1,0,2:T(8,128)(2,1)} fusion(bf16[3,4,2,4,256,128]{5,4,3,1,0,2:T(8,128)(2,1)} %bitcast.174, pred[3,4]{1,0:T(4,128)(4,1)S(1)} %get-tuple-element.12), kind=kLoop, calls=%fused_computation.8 | loop fusion | flops 3145728 | bytes 12582924 | tf_op jit(solution)/shard_map/jit(take_along_axis)/select_n | solution.py:113
  104.7 3.8 %all-to-all-done = bf16[16,12,512]{2,1,0:T(8,128)(2,1)S(1)} async-done(((bf16[16,12,512]{2,1,0:T(8,128)(2,1)}), bf16[16,12,512]{2,1,0:T(8,128)(2,1)S(1)}, u32[]{:S(2)}, u32[]{:S(2)}) %all-to-all-start) | async-done | bytes 196640 | tf_op jit(solution)/shard_map/all_to_all | solution.py:101
  108.6 1.0 copy.50
  109.6 1.0 reshape.190
  110.6 1.0 multiply_subtract_fusion
  111.8 0.9 fusion.58
  112.7 2.9 %select_reduce_fusion = (f32[3,4,4,16]{3,2,1,0:T(4,128)S(1)}, f32[3,4,4,16,256]{4,3,2,1,0:T(8,128)S(1)}) fusion(pred[3,4,256]{2,1,0:T(4,128)(4,1)S(1)} %iota_compare_fusion, bf16[3,4,2,4,256,128]{5,4,3,1,0,2:T(8,128)(2,1)} %broadcast_select_fusion.2, bf16[3,4,4,16,128]{4,3,1,2,0:T(8,128)(2,1)S(1)} %fusion.56), kind=kOutput, calls=%fused_computation.39 | convolution fusion | flops 50724096 | bytes 4134912 | tf_op jit(solution)/shard_map/pbkge,pbkse->pbkgs/dot_general | solution.py:55
  116.1 1.3 bitcast_reduce_fusion
  117.4 0.7 fusion.12
  118.1 0.5 slice-done.1
  118.6 0.5 fusion.21
  119.2 1.2 fusion.49
  120.7 12.8 %all_to_all.24 = bf16[12,16,512]{2,0,1:T(8,128)(2,1)S(1)} all-to-all(bf16[12,16,512]{2,0,1:T(8,128)(2,1)S(1)} %copy.61), channel_id=1, replica_groups=mesh['groups'=2,'tensor'=16] {'tensor'}, dimensions={1} | all-to-all | bytes 393216 | tf_op jit(solution)/shard_map/all_to_all | solution.py:133
  133.6 11.9 %convolution_convert_fusion = bf16[192,16384]{1,0:T(8,128)(2,1)} fusion(bf16[192,512]{1,0:T(8,128)(2,1)S(1)} %all_to_all.21, bf16[512,16384]{1,0:T(8,128)(2,1)} %param.10), kind=kOutput, calls=%fused_computation.2 | convolution fusion | flops 3224371200 | bytes 23265280 | tf_op jit(solution)/shard_map/dot_general | solution.py:134
  145.5 83.7 %reduce-scatter.2.cloned.1.call-done = bf16[192,1024]{1,0:T(8,128)(2,1)} async-done(((bf16[192,16384]{1,0:T(8,128)(2,1)}), bf16[192,1024]{1,0:T(8,128)(2,1)}) %reduce-scatter.2.cloned.1.call-update) | async-done | bytes 393232 | tf_op jit(solution)/shard_map/reduce_scatter | solution.py:135
  (49 shorter events, 2.3 us)
Async XLA Ops:
  6.5 15.9 %copy-start = (bf16[1,3,2,4,512,128]{5,4,3,2,1,0:T(8,128)(2,1)S(1)}, bf16[1,3,2,4,512,128]{5,4,3,2,1,0:T(8,128)(2,1)}, u32[]{:S(2)}) copy-start(bf16[1,3,2,4,512,128]{5,4,3,2,1,0:T(8,128)(2,1)} %param.12) | copy-start | bytes 9437188
  6.5 5.3 %copy-start.6 = (s32[12]{0:T(128)S(1)}, s32[12]{0:T(128)}, u32[]{:S(2)}) copy-start(s32[12]{0:T(128)} %param.15) | copy-start | bytes 148
  6.5 5.6 %copy-start.5 = (s32[12]{0:T(128)S(1)}, s32[12]{0:T(128)}, u32[]{:S(2)}) copy-start(s32[12]{0:T(128)} %param.14) | copy-start | bytes 148
  6.5 5.9 %copy-start.3 = (bf16[12,2,4,128]{3,2,1,0:T(4,128)(2,1)S(1)}, bf16[12,2,4,128]{3,2,1,0:T(4,128)(2,1)}, u32[]{:S(2)}) copy-start(bf16[12,2,4,128]{3,2,1,0:T(4,128)(2,1)} %param.11) | copy-start | bytes 73732
  6.5 67.7 %all-gather.2.cloned.1.call-start = ((), (), s32[]{:S(2)}) async-start(), calls=%async_computation.3 | async-start | bytes 6684672 | tf_op jit(solution)/shard_map/all_gather | solution.py:95
  7.3 20.2 %collective-permute-start.2 = (bf16[12,2,4,256,128]{4,3,2,1,0:T(8,128)(2,1)}, bf16[12,2,4,256,128]{4,3,2,1,0:T(8,128)(2,1)}, u32[]{:S(2)}, u32[]{:S(2)}) collective-permute-start(bf16[12,2,4,256,128]{4,3,2,1,0:T(8,128)(2,1)} %param.13), channel_id=1, source_target_pairs={{0,1},{1,0},{2,3},{3,2},{4,5},{5,4},{6,7},{7,6},{8,9},{9,8},{10,11... | collective-permute-start | bytes 18874376 | tf_op jit(solution)/shard_map/ppermute | solution.py:21
  11.6 10.8 %collective-permute-start = (bf16[1,3,2,4,512,128]{5,4,3,1,2,0:T(8,128)(2,1)}, bf16[1,3,2,4,512,128]{5,4,3,1,2,0:T(8,128)(2,1)}, u32[]{:S(2)}, u32[]{:S(2)}) collective-permute-start(bf16[1,3,2,4,512,128]{5,4,3,1,2,0:T(8,128)(2,1)} %copy.48), channel_id=1, source_target_pairs={{0,1},{1,0},{2,3},{3,2},{4,5},{5,4},{6,7},{7,6},{8,9},{9,8},{10,11... | collective-permute-start | bytes 9437192 | tf_op jit(solution)/shard_map/ppermute | solution.py:21
  11.8 5.7 %collective-permute-start.1 = (s32[12]{0:T(128)S(1)}, s32[12]{0:T(128)S(1)}, u32[]{:S(2)}, u32[]{:S(2)}) collective-permute-start(s32[12]{0:T(128)S(1)} %copy-done.6), channel_id=1, source_target_pairs={{0,1},{1,0},{2,3},{3,2},{4,5},{5,4},{6,7},{7,6},{8,9},{9,8},{10,11... | collective-permute-start | bytes 152 | tf_op jit(solution)/shard_map/ppermute | solution.py:21
  18.7 8.7 %slice-start.2 = ((s8[6291456]{0:T(1024)(128)(4,1)}), s8[4194304]{0:T(1024)(128)(4,1)S(1)}, s32[]{:S(2)}) async-start(s8[6291456]{0:T(1024)(128)(4,1)} %bitcast.179), calls=%async_computation.7 | async-start | bytes 8388608
  19.5 8.0 %slice-start.3 = ((s8[6291456]{0:T(1024)(128)(4,1)}), s8[2097152]{0:T(1024)(128)(4,1)S(1)}, s32[]{:S(2)}) async-start(s8[6291456]{0:T(1024)(128)(4,1)} %bitcast.179), calls=%async_computation.8 | async-start | bytes 4194304
  95.0 13.5 %all-to-all-start = ((bf16[16,12,512]{2,1,0:T(8,128)(2,1)}), bf16[16,12,512]{2,1,0:T(8,128)(2,1)S(1)}, u32[]{:S(2)}, u32[]{:S(2)}) async-start(bf16[16,12,512]{2,1,0:T(8,128)(2,1)} %constant_dynamic-update-slice_fusion), calls=%async_computation | async-start | bytes 524288 | tf_op jit(solution)/shard_map/all_to_all | solution.py:101
  98.5 130.6 %reduce-scatter.2.cloned.1.call-start = ((), (), s32[]{:S(2)}) async-start(), calls=%async_computation.4 | async-start | bytes 6684672 | tf_op jit(solution)/shard_map/reduce_scatter | solution.py:135
  104.7 11.3 %copy-start.1 = (bf16[3,2,4,512,128]{4,3,2,0,1:T(8,128)(2,1)S(1)}, bf16[3,2,4,512,128]{4,3,2,0,1:T(8,128)(2,1)}, u32[]{:S(2)}) copy-start(bf16[3,2,4,512,128]{4,3,2,0,1:T(8,128)(2,1)} %get-tuple-element.15) | copy-start | bytes 9437188
  110.6 5.4 %copy-start.2 = (bf16[3,2,4,512,128]{4,3,2,0,1:T(8,128)(2,1)S(1)}, bf16[3,2,4,512,128]{4,3,2,0,1:T(8,128)(2,1)}, u32[]{:S(2)}) copy-start(bf16[3,2,4,512,128]{4,3,2,0,1:T(8,128)(2,1)} %get-tuple-element.16) | copy-start | bytes 9437188
  115.6 2.5 %slice-start = ((s8[6291456]{0:T(1024)(128)(4,1)}), s8[4194304]{0:T(1024)(128)(4,1)S(1)}, s32[]{:S(2)}) async-start(s8[6291456]{0:T(1024)(128)(4,1)} %bitcast.177), calls=%async_computation.5 | async-start | bytes 8388608
  116.0 2.6 %slice-start.1 = ((s8[6291456]{0:T(1024)(128)(4,1)}), s8[2097152]{0:T(1024)(128)(4,1)S(1)}, s32[]{:S(2)}) async-start(s8[6291456]{0:T(1024)(128)(4,1)} %bitcast.177), calls=%async_computation.6 | async-start | bytes 4194304
  117.4 1.8 copy-start.4
Sparse Core Ops, SparseCore 0:
  9.6 64.6 all-gather.1
  145.6 83.5 reduce-scatter.1
